TPU v7x, 32 devices: a whole 2x2x4 slice. The times are simulated.
32 devices in a mesh: parts: 2 (over y), freq: 4 (over z), pan: 2 (over x), rep: 2 (over core).
Axes of the slice: x: 2, y: 2, z: 4, core: 2. Of those that a mesh axis runs over, the one named last changes fastest.
Arguments:
- traces: bfloat16 [2048, 4096], P(('parts', 'freq', 'pan', 'rep')), parts along dimension 0, may hold values from -6 to 6
- data: bfloat16 [8, 2, 2048, 2048], P(('parts', 'freq'), None, ('pan', 'rep')), parts along dimension 0, may hold values from -1.5 to 1.5
- trace_shot: int32 [2048], P('parts'), parts along dimension 0, may hold values from 0 to 2047, as said below
- trace_recv: int32 [2048], P('parts'), parts along dimension 0, may hold values from 0 to 2047
- aper_panel: int32 [8, 4], P('parts'), parts along dimension 0, may hold values from 0 to 15
- aper_order: int32 [8, 4], P('parts'), parts along dimension 0, may hold values from 0 to 3, each once within a row
- aper_count: int32 [8], P('parts'), parts along dimension 0, may hold values from 1 to 4, as said below
Outputs:
- multiples: bfloat16 [8, 2, 2048, 2048], P(('parts', 'freq'), None, ('pan', 'rep')), parts along dimension 0
- primaries: float32 [2048, 2, 4], P(('parts', 'freq', 'pan', 'rep')), parts along dimension 0
There are 2 independent parts, one for each index of `parts`. A program takes and returns all parts, laid end to end along the dimension named above; each array names one. Nothing has to cross between parts.
Inputs may be any that keep to these rules, and one draw needn't show every extreme that they name: `trace_shot`: among the 64 traces of each aligned block (one device's traces), at most 32 have shots of one group of 512 shots, and some group has exactly 32. `aper_count`: some group's aperture takes all 4 groups.
All inputs are finite; a program needn't handle non-finite values.
Results may differ from a plain program's by a relative error of at most 0.0034.
Values may be sent and summed in bfloat16 or wider, within the bound.
A program may use at most 192 MiB of HBM per device.

v0:
```python
import math

import jax
import jax.numpy as jnp
from jax import lax
from jax.sharding import PartitionSpec as P

KB = 32
FBIN0 = 64
FSTEP = 3


def spectral_table(samples, count, first, stride):
    times = jnp.arange(samples, dtype=jnp.int32)
    bins = first + stride * jnp.arange(count, dtype=jnp.int32)
    phase = times[:, None] * bins[None, :] % samples
    angle = phase.astype(jnp.float32) * (2.0 * math.pi / samples)
    factor = 1.0 / math.sqrt(samples)
    return jnp.concatenate([jnp.cos(angle) * factor, -jnp.sin(angle) * factor], axis=1).astype(
        jnp.bfloat16
    )


def membership(order, counts):
    width = order.shape[0]
    position = jnp.arange(width, dtype=jnp.int32)
    within = position[None, :] < counts[:, None]
    hits = (order[:, :, None] == position[None, None, :]) & within[:, :, None]
    return jnp.any(hits, axis=1).astype(jnp.float32)


def route_ranks(shots, block_size, group_count, group_width):
    target_group = shots // group_width
    onehot = (target_group[:, None] == jnp.arange(group_count, dtype=jnp.int32)[None, :]).astype(
        jnp.int32
    )
    onehot = onehot.reshape(-1, block_size, group_count)
    before = jnp.cumsum(onehot, axis=1) - onehot
    ranking = jnp.sum(before * onehot, axis=2).reshape(-1)
    return (target_group, ranking)


def local(traces, data, trace_shot, trace_recv, aper_panel, aper_order, aper_count):
    band_count = lax.axis_size("freq")
    reader_count = lax.axis_size(("pan", "rep"))
    freq_local = data.shape[0]
    shot_width = data.shape[2]
    matrix_order = data.shape[3]
    trace_local = traces.shape[0]
    capacity = 2 * trace_local // reader_count
    slot_total = reader_count * band_count * capacity
    freq_total = freq_local * band_count
    panel_local = shot_width // KB
    reader = lax.axis_index(("pan", "rep"))
    source = lax.axis_index(("freq", "pan", "rep"))
    chosen = aper_panel[:, reader]
    strips = data.reshape(freq_local, 2, panel_local, KB, matrix_order)
    outgoing = jnp.take(strips, chosen, axis=2)
    arrived_panels = lax.all_to_all(
        outgoing, ("pan", "rep"), split_axis=2, concat_axis=2, tiled=True
    )
    table = spectral_table(traces.shape[1], freq_total, FBIN0, FSTEP)
    spectrum = jnp.dot(traces, table, preferred_element_type=jnp.float32).astype(jnp.bfloat16)
    spectrum = spectrum.reshape(trace_local, 2, freq_total)
    own_shots = lax.dynamic_slice_in_dim(trace_shot, source * trace_local, trace_local)
    own_group, own_rank = route_ranks(own_shots, trace_local, reader_count, shot_width)
    own_slot = own_group * capacity + own_rank
    used = membership(aper_order, aper_count)[reader]
    mine_panel = aper_panel[reader]
    owners = jnp.arange(reader_count, dtype=jnp.int32)
    columns = (
        (owners * panel_local + mine_panel)[:, None] * KB + jnp.arange(KB, dtype=jnp.int32)[None, :]
    ).reshape(-1)
    live_cols = jnp.repeat(used, KB).astype(jnp.bfloat16)
    taken = jnp.take(data, columns, axis=3)
    left_real = taken[:, 0] * live_cols
    left_imag = taken[:, 1] * live_cols
    panel_real = arrived_panels[:, 0].reshape(freq_local, reader_count * KB, matrix_order)
    panel_imag = arrived_panels[:, 1].reshape(freq_local, reader_count * KB, matrix_order)
    real_part = jnp.einsum(
        "fsk,fkn->fsn", left_real, panel_real, preferred_element_type=jnp.float32
    )
    real_part = real_part - jnp.einsum(
        "fsk,fkn->fsn", left_imag, panel_imag, preferred_element_type=jnp.float32
    )
    imag_part = jnp.einsum(
        "fsk,fkn->fsn", left_real, panel_imag, preferred_element_type=jnp.float32
    )
    imag_part = imag_part + jnp.einsum(
        "fsk,fkn->fsn", left_imag, panel_real, preferred_element_type=jnp.float32
    )
    multiples = jnp.stack([real_part, imag_part], axis=1).astype(jnp.bfloat16)
    every_group, every_rank = route_ranks(trace_shot, trace_local, reader_count, shot_width)
    source_of = jnp.arange(trace_shot.shape[0], dtype=jnp.int32) // trace_local
    band_of = source_of // reader_count
    owner_of = source_of % reader_count
    target = jnp.where(
        every_group == reader, (owner_of * band_count + band_of) * capacity + every_rank, slot_total
    )
    slot_shot = (
        jnp.zeros((slot_total,), jnp.int32)
        .at[target]
        .set(trace_shot - reader * shot_width, mode="drop")
    )
    slot_recv = jnp.zeros((slot_total,), jnp.int32).at[target].set(trace_recv, mode="drop")
    slot_live = jnp.zeros((slot_total,), jnp.float32).at[target].set(1.0, mode="drop")
    picked = jnp.transpose(multiples[:, :, slot_shot, slot_recv], (2, 1, 0)).astype(jnp.float32)
    picked = picked * slot_live[:, None, None]
    selector = (
        jnp.arange(reader_count * capacity, dtype=jnp.int32)[:, None] == own_slot[None, :]
    ).astype(jnp.bfloat16)
    buckets = jnp.einsum(
        "jt,tcf->jcf", selector, spectrum, preferred_element_type=jnp.float32
    ).astype(jnp.bfloat16)
    buckets = buckets.reshape(reader_count, capacity, 2, freq_total)
    arrived = lax.all_to_all(
        lax.all_to_all(buckets, "freq", split_axis=3, concat_axis=1, tiled=True),
        ("pan", "rep"),
        split_axis=0,
        concat_axis=1,
        tiled=True,
    )
    difference = arrived[0].astype(jnp.float32) - picked
    difference = difference.reshape(reader_count, band_count, capacity, 2, freq_local)
    returned = lax.all_to_all(
        lax.all_to_all(difference, "freq", split_axis=1, concat_axis=4, tiled=True),
        ("pan", "rep"),
        split_axis=0,
        concat_axis=1,
        tiled=True,
    )
    values = returned.reshape(reader_count * capacity, 2, freq_total)
    primaries = jnp.take(values, own_slot, axis=0)
    return (multiples, primaries)


def solution(mesh):
    in_specs = (
        P(("parts", "freq", "pan", "rep"), None),
        P(("parts", "freq"), None, ("pan", "rep"), None),
        P("parts"),
        P("parts"),
        P("parts", None),
        P("parts", None),
        P("parts"),
    )
    out_specs = (
        P(("parts", "freq"), None, ("pan", "rep"), None),
        P(("parts", "freq", "pan", "rep"), None, None),
    )
    return jax.shard_map(local, mesh=mesh, in_specs=in_specs, out_specs=out_specs, check_vma=False)
```

profile of v0, /device:TPU:0, one launch (start us, length us, event | category | flops | bytes accessed | tf_op | source)
XLA Modules:
  0.0 109.5 jit_solution(8782309627390931492)
XLA Ops:
  0.7 0.8 and_select_fusion
  1.7 0.2 select_reduce_fusion.1
  1.8 0.8 compare_and_fusion
  2.6 0.6 multiply_convert_fusion.1
  3.3 0.4 fusion.3
  3.7 0.7 reshape.460
  4.4 6.3 %all-to-all-start.1 = ((bf16[4,2,128]{2,1,0:T(2,128)(2,1)}), bf16[4,2,128]{2,1,0:T(2,128)(2,1)S(1)}, u32[]{:S(2)}, u32[]{:S(2)}) async-start(bf16[4,2,128]{2,1,0:T(2,128)(2,1)} %reshape.460), calls=%async_computation.1 | async-start | bytes 4096 | tf_op jit(solution)/shard_map/all_to_all | solution.py:117
  10.7 0.7 fusion.61
  11.6 0.9 fusion.58
  12.5 0.9 and_reduce_fusion
  13.4 0.7 add_select_fusion.4
  14.1 11.1 %copy.53 = bf16[1,2,512,2048]{2,1,3,0:T(2,128)(2,1)} copy(bf16[1,2,512,2048]{3,2,1,0:T(8,128)(2,1)} %param.8) | data formatting | bytes 8388608 | tf_op args[1]
  25.8 1.4 %select_reduce_fusion = s32[16,64]{0,1:T(8,128)S(1)} fusion(s32[16,64]{0,1:T(8,128)S(1)} %copy.59), kind=kOutput, calls=%fused_computation.19 | output fusion | flops 285696 | bytes 8192 | tf_op jit(solution)/shard_map/jit(cumsum)/reduce_window_sum | solution.py:38
  27.2 3.3 %gather_fusion = bf16[128,2,512]{2,1,0:T(2,128)(2,1)S(1)} fusion(bf16[2,512,2048]{1,0,2:T(2,128)(2,1)} %bitcast.100, s32[1024]{0:T(1024)S(1)} %pad_clamp_fusion.2), kind=kCustom, calls=%fused_computation | custom fusion | bytes 524800 | tf_op jit(solution)/shard_map/jit(_take)/gather | solution.py:75
  30.6 0.3 broadcast_select_fusion
  30.9 2.8 %gather_fusion.1 = bf16[4,2,32,2048]{3,2,1,0:T(8,128)(2,1)S(1)} fusion(bf16[2,16,32,2048]{3,2,1,0:T(8,128)(2,1)} %bitcast.99, s32[1024]{0:T(1024)S(1)} %pad_clamp_fusion.1), kind=kCustom, calls=%fused_computation.1 | custom fusion | bytes 2097168 | tf_op jit(solution)/shard_map/jit(_take)/gather | solution.py:58
  33.7 1.1 %bitcast_select_fusion = bf16[1,2,4,32,2048]{4,3,1,0,2:T(8,128)(2,1)} fusion(bf16[4,2,32,2048]{3,2,1,0:T(8,128)(2,1)S(1)} %gather_fusion.1, pred[4]{0:T(512)(128)(4,1)S(1)} %and_reduce_fusion), kind=kLoop, calls=%fused_computation.15 | loop fusion | flops 524288 | bytes 2097156 | tf_op jit(solution)/shard_map/jit(_take)/select_n | solution.py:58
  34.9 0.6 slice_multiply_fusion
  35.5 0.2 copy.54
  35.7 0.2 copy.55
  36.0 3.5 %all-to-all-start = ((bf16[1,2,4,32,2048]{4,3,1,0,2:T(8,128)(2,1)}), bf16[1,2,4,32,2048]{4,3,1,0,2:T(8,128)(2,1)S(1)}, u32[]{:S(2)}, u32[]{:S(2)}) async-start(bf16[1,2,4,32,2048]{4,3,1,0,2:T(8,128)(2,1)} %bitcast_select_fusion), calls=%async_computation | async-start | bytes 2097152 | tf_op jit(solution)/shard_map/all_to_all | solution.py:59
  39.6 4.3 %scatter_custom_fusion = s32[512]{0:T(512)S(1)} fusion(s32[1024]{0:T(1024)S(1)} %get-tuple-element.19, s32[1024]{0:T(1024)S(1)} %get-tuple-element.18, s32[]{:T(128)} %constant.138.clone.1), kind=kCustom, calls=%fused_computation.110 | custom fusion | bytes 2052 | tf_op jit(solution)/shard_map/scatter | solution.py:103
  43.9 4.5 %scatter_custom_fusion.1 = s32[512]{0:T(512)S(1)} fusion(s32[1024]{0:T(1024)S(1)} %get-tuple-element.19, s32[1024]{0:T(1024)} %param.10, s32[]{:T(128)} %constant.138.clone.1), kind=kCustom, calls=%fused_computation.112 | custom fusion | bytes 2560 | tf_op jit(solution)/shard_map/scatter | solution.py:105
  48.4 4.3 %scatter_custom_fusion.2 = f32[512]{0:T(512)S(1)} fusion(s32[1024]{0:T(1024)S(1)} %get-tuple-element.19, f32[1024]{0:T(1024)S(1)} %broadcast.280, f32[]{:T(128)} %constant.164.clone.1), kind=kCustom, calls=%fused_computation.114 | custom fusion | bytes 2052 | tf_op jit(solution)/shard_map/scatter | solution.py:106
  52.8 0.7 all_to_all.47
  53.5 0.5 all-to-all-done
  54.0 3.4 %all-to-all-start.2 = ((bf16[4,128,2,1]{1,2,3,0:T(2,128)(2,1)}), bf16[4,128,2,1]{1,2,3,0:T(2,128)(2,1)S(1)}, u32[]{:S(2)}, u32[]{:S(2)}) async-start(bf16[4,128,2,1]{1,2,3,0:T(2,128)(2,1)} %bitcast.21), calls=%async_computation.2 | async-start | bytes 4096 | tf_op jit(solution)/shard_map/all_to_all | solution.py:116
  57.5 0.7 fusion.13
  58.2 0.7 fusion.11
  58.9 0.7 fusion
  59.6 0.7 fusion.1
  60.3 1.3 %copy-done.1 = bf16[1,1,512,2048]{3,2,1,0:T(8,128)(2,1)} copy-done((bf16[1,1,512,2048]{3,2,1,0:T(8,128)(2,1)}, bf16[1,1,512,2048]{3,2,1,0:T(8,128)(2,1)S(1)}, u32[]{:S(2)}) %copy-start.1) | copy-done | bytes 2097176
  61.6 2.4 %fusion.73 = bf16[2,512,2048]{2,1,0:T(8,128)(2,1)} fusion(bf16[1,1,512,2048]{3,2,1,0:T(8,128)(2,1)S(1)} %fusion.1, bf16[1,1,512,2048]{3,2,1,0:T(8,128)(2,1)S(1)} %fusion), kind=kLoop, calls=%fused_computation.134 | loop fusion | flops 2097152 | bytes 8388608 | tf_op jit(solution)/shard_map/stack | solution.py:92
  64.0 8.4 %copy.61 = bf16[2,512,2048]{2,0,1:T(2,128)(2,1)} copy(bf16[2,512,2048]{2,1,0:T(8,128)(2,1)} %fusion.73) | data formatting | bytes 8388608 | tf_op jit(solution)/shard_map/stack | solution.py:92
  72.4 13.4 %gather_fusion.2 = bf16[512,2]{0,1:T(2,128)(2,1)S(1)} fusion(bf16[2,512,2048]{2,0,1:T(2,128)(2,1)} %copy.61, s32[512]{0:T(512)S(1)} %fusion.49), kind=kCustom, calls=%fused_computation.2 | custom fusion | bytes 8192 | tf_op jit(solution)/shard_map/gather | solution.py:107
  86.0 0.7 reshape.462
  86.7 5.1 %all-to-all-start.3 = ((f32[4,1,256]{2,1,0:T(1,128)}), f32[4,1,256]{2,1,0:T(1,128)S(1)}, u32[]{:S(2)}, u32[]{:S(2)}) async-start(f32[4,1,256]{2,1,0:T(1,128)} %reshape.462), calls=%async_computation.3 | async-start | bytes 8192 | tf_op jit(solution)/shard_map/all_to_all | solution.py:126
  91.8 5.6 %all-to-all-done.3 = f32[4,1,256]{2,1,0:T(1,128)S(1)} async-done(((f32[4,1,256]{2,1,0:T(1,128)}), f32[4,1,256]{2,1,0:T(1,128)S(1)}, u32[]{:S(2)}, u32[]{:S(2)}) %all-to-all-start.3) | async-done | bytes 4128 | tf_op jit(solution)/shard_map/all_to_all | solution.py:126
  97.4 0.6 broadcast.343
  97.9 0.7 reduce.5
  98.8 0.7 reshape.464
  99.4 3.6 %all-to-all-start.4 = ((f32[4,1,256]{2,1,0:T(1,128)}), f32[4,1,256]{2,1,0:T(1,128)S(1)}, u32[]{:S(2)}, u32[]{:S(2)}) async-start(f32[4,1,256]{2,1,0:T(1,128)} %reshape.464), calls=%async_computation.4 | async-start | bytes 8192 | tf_op jit(solution)/shard_map/all_to_all | solution.py:125
  103.0 4.0 %pad_maximum_fusion = bf16[1,2,512,2048]{3,2,1,0:T(8,128)(2,1)} fusion(bf16[1,1,512,2048]{3,2,1,0:T(8,128)(2,1)} %copy-done.1, bf16[1,1,512,2048]{3,2,1,0:T(8,128)(2,1)S(1)} %fusion), kind=kLoop, calls=%fused_computation.7 | loop fusion | flops 2097152 | bytes 8388608 | tf_op jit(solution)/shard_map/stack | solution.py:92
  107.0 0.7 reduce.6
  107.8 0.1 copy.67
  108.0 0.7 gather_fusion.3
  108.6 0.1 broadcast_select_fusion.1
  108.8 0.7 copy.66
  (51 shorter events, 1.7 us)
Async XLA Ops:
  0.6 2.6 %copy-start = (bf16[64,4096]{1,0:T(8,128)(2,1)S(1)}, bf16[64,4096]{1,0:T(8,128)(2,1)}, u32[]{:S(2)}) copy-start(bf16[64,4096]{1,0:T(8,128)(2,1)} %param.7) | copy-start | bytes 1572868
  4.4 31.6 %all-to-all-start.1 = ((bf16[4,2,128]{2,1,0:T(2,128)(2,1)}), bf16[4,2,128]{2,1,0:T(2,128)(2,1)S(1)}, u32[]{:S(2)}, u32[]{:S(2)}) async-start(bf16[4,2,128]{2,1,0:T(2,128)(2,1)} %reshape.460), calls=%async_computation.1 | async-start | bytes 4096 | tf_op jit(solution)/shard_map/all_to_all | solution.py:117
  14.1 11.2 %copy-start.4 = (s32[4]{0:T(128)S(1)}, s32[4]{0:T(128)}, u32[]{:S(2)}) copy-start(s32[4]{0:T(128)} %param.13) | copy-start | bytes 52
  14.1 11.2 %copy-start.3 = (s32[4,4]{1,0:T(4,128)S(1)}, s32[4,4]{1,0:T(4,128)}, u32[]{:S(2)}) copy-start(s32[4,4]{1,0:T(4,128)} %param.12) | copy-start | bytes 196
  30.9 8.7 %copy-start.2 = (s32[1024]{0:T(1024)S(1)}, s32[1024]{0:T(1024)}, u32[]{:S(2)}) copy-start(s32[1024]{0:T(1024)} %param.9) | copy-start | bytes 12292
  36.0 18.0 %all-to-all-start = ((bf16[1,2,4,32,2048]{4,3,1,0,2:T(8,128)(2,1)}), bf16[1,2,4,32,2048]{4,3,1,0,2:T(8,128)(2,1)S(1)}, u32[]{:S(2)}, u32[]{:S(2)}) async-start(bf16[1,2,4,32,2048]{4,3,1,0,2:T(8,128)(2,1)} %bitcast_select_fusion), calls=%async_computation | async-start | bytes 2097152 | tf_op jit(solution)/shard_map/all_to_all | solution.py:59
  54.0 31.9 %all-to-all-start.2 = ((bf16[4,128,2,1]{1,2,3,0:T(2,128)(2,1)}), bf16[4,128,2,1]{1,2,3,0:T(2,128)(2,1)S(1)}, u32[]{:S(2)}, u32[]{:S(2)}) async-start(bf16[4,128,2,1]{1,2,3,0:T(2,128)(2,1)} %bitcast.21), calls=%async_computation.2 | async-start | bytes 4096 | tf_op jit(solution)/shard_map/all_to_all | solution.py:116
  60.3 1.3 %copy-start.1 = (bf16[1,1,512,2048]{3,2,1,0:T(8,128)(2,1)}, bf16[1,1,512,2048]{3,2,1,0:T(8,128)(2,1)S(1)}, u32[]{:S(2)}) copy-start(bf16[1,1,512,2048]{3,2,1,0:T(8,128)(2,1)S(1)} %fusion.1) | copy-start | bytes 6291460
  86.7 10.7 %all-to-all-start.3 = ((f32[4,1,256]{2,1,0:T(1,128)}), f32[4,1,256]{2,1,0:T(1,128)S(1)}, u32[]{:S(2)}, u32[]{:S(2)}) async-start(f32[4,1,256]{2,1,0:T(1,128)} %reshape.462), calls=%async_computation.3 | async-start | bytes 8192 | tf_op jit(solution)/shard_map/all_to_all | solution.py:126
  99.4 7.6 %all-to-all-start.4 = ((f32[4,1,256]{2,1,0:T(1,128)}), f32[4,1,256]{2,1,0:T(1,128)S(1)}, u32[]{:S(2)}, u32[]{:S(2)}) async-start(f32[4,1,256]{2,1,0:T(1,128)} %reshape.464), calls=%async_computation.4 | async-start | bytes 8192 | tf_op jit(solution)/shard_map/all_to_all | solution.py:125
where the time goes:
time: 112 us; the launch traced here: 109 us
  local copies, waits for them, and re-layouts  59.9 us (53%)
  starting transfers between devices  21.9 us (20%)
  other arithmetic  17.5 us (16%)
  waiting for transfers between devices  6.07 us (5%)
  matrix products  3.15 us (3%)
    unnamed x18, local copies, waits for them, and re-layouts  15.5 us
    gather x1, local copies, waits for them, and re-layouts, local(): multiples[:, :, slot_shot, slot_recv]  13.4 us
    another operation x1, local copies, waits for them, and re-layouts, local(): multiples = jnp.stack([real_part, imag_part], axis=1).astype(jnp.bfloat16)  8.42 us
    another operation x2, other arithmetic, local(): multiples = jnp.stack([real_part, imag_part], axis=1).astype(jnp.bfloat16)  6.36 us
    all_to_all x1, starting transfers between devices, local(): lax.all_to_all(buckets, 'freq', split_axis=3, concat_axis=1, tiled=True)  6.32 us
    all_to_all x1, waiting for transfers between devices, local(): lax.all_to_all(difference, 'freq', split_axis=1, concat_axis=4, tiled=True)  5.57 us
    all_to_all x1, starting transfers between devices, local(): lax.all_to_all(difference, 'freq', split_axis=1, concat_axis=4, tiled=True)  5.09 us
    scatter x1, local copies, waits for them, and re-layouts, local(): jnp.zeros((slot_total,), jnp.int32).at[target].set(trace_recv, mode='drop')  4.46 us
  transfers between devices with their start and end apart: 5, of which 2 were waited for; matrix products, arithmetic and copies ran while one was open for 63% of the time, Pallas kernels for 0%

commit v1 on v0

v1 whole, which is shorter than its diff:
```python
import functools
import math

import jax
import jax.numpy as jnp
import numpy as np
from jax import lax
from jax.experimental import pallas as pl
from jax.experimental.pallas import tpu as pltpu
from jax.sharding import PartitionSpec as P

KB = 32
FBIN0 = 64
FSTEP = 3
LANES = 128
CHUNKS = 4
BLOCK = 2 * LANES
MESH = pl.DeviceIdType.MESH
BF = jnp.bfloat16
F32 = jnp.float32


def spectral_table(samples, count, first, stride):
    times = np.arange(samples, dtype=np.int32)
    bins = first + stride * np.arange(count, dtype=np.int32)
    phase = bins[:, None] * times[None, :] % samples
    angle = phase.astype(np.float32) * np.float32(2.0 * math.pi / samples)
    factor = np.float32(1.0 / math.sqrt(samples))
    rows = np.concatenate([np.cos(angle) * factor, -np.sin(angle) * factor], axis=0)
    padded = np.zeros((-(-rows.shape[0] // 16) * 16, samples), np.float32)
    padded[: rows.shape[0]] = rows
    return padded.astype(jnp.bfloat16)


def kernel(
    sizes,
    data_hbm, traces_hbm, table_hbm, panel_s, order_s, count_s, shot_v, recv_v,
    out_hbm, prim_v,
    data_v, traces_v, table_v, send, panels, sel, left_a, left_b, left_t, hot, lsel, acc, picks,
    arrived, tidy, stage,
    load_sem, send_sem, recv_sem, pick_send, pick_recv, out_sem,
):
    NF, PAN, REP, SW, NS, TL, GROUP = sizes
    R = PAN * REP
    N = NF * R
    RK = R * KB
    W = NS // CHUNKS
    PB = LANES // TL
    freq, pan, rep = lax.axis_index("freq"), lax.axis_index("pan"), lax.axis_index("rep")
    reader = pan * REP + rep
    me = freq * R + reader

    def place(s):
        r = lax.rem(s, R)
        return {"freq": lax.div(s, R), "pan": lax.div(r, REP), "rep": lax.rem(r, REP)}

    loads = [
        pltpu.make_async_copy(data_hbm.at[0], data_v, load_sem.at[0]),
        pltpu.make_async_copy(traces_hbm, traces_v, load_sem.at[1]),
        pltpu.make_async_copy(table_hbm, table_v, load_sem.at[2]),
    ]
    for copy in loads:
        copy.start()

    barrier = pltpu.get_barrier_semaphore()

    @pl.loop(1, N)
    def _(k):
        pl.semaphore_signal(
            barrier, inc=1, device_id=place(lax.rem(me + k, N)), device_id_type=MESH
        )

    loads[0].wait()
    offsets = [(dp, dr) for dp in range(PAN) for dr in range(REP) if (dp, dr) != (0, 0)]
    offsets = [o for o in offsets if o[0]] + [o for o in offsets if not o[0]]

    for n, (dp, dr) in enumerate(offsets):
        p = panel_s[lax.rem(pan + dp, PAN) * REP + lax.rem(rep + dr, REP), reader]
        for c in range(CHUNKS):
            send[n, c] = data_v[:, p, :, c * W : (c + 1) * W]
    pl.semaphore_wait(barrier, N - 1)

    def panel_copy(n, c, slot):
        dp, dr = offsets[n]
        return pltpu.make_async_remote_copy(
            src_ref=send.at[n, c],
            dst_ref=panels.at[c, :, slot],
            send_sem=send_sem.at[n, c],
            recv_sem=recv_sem.at[n, c],
            device_id={"pan": lax.rem(pan + dp, PAN), "rep": lax.rem(rep + dr, REP)},
            device_id_type=MESH,
        )

    for c in range(CHUNKS):
        for n in range(R - 1):
            panel_copy(n, c, reader).start()
    p = panel_s[reader, reader]
    for c in range(CHUNKS):
        panels[c, :, reader] = data_v[:, p, :, c * W : (c + 1) * W]

    lane = lax.broadcasted_iota(jnp.int32, (1, RK), 1)
    column = jnp.full((1, RK), -1, jnp.int32)
    for q in range(R):
        hit = jnp.int32(0)
        for m in range(R):
            named = (order_s[reader, m] == q).astype(jnp.int32)
            hit = hit + named * (count_s[reader] > m).astype(jnp.int32)
        base = hit * (q * SW + panel_s[reader, q] * KB - q * KB + 2 * NS) - 2 * NS
        column = jnp.where((lane >= q * KB) & (lane < (q + 1) * KB), lane + base, column)

    @pl.loop(0, NS // 256)
    def _(b):
        at = pl.multiple_of(b * 256, 256)
        rows = lax.broadcasted_iota(jnp.int32, (256, RK), 0) + at
        sel[pl.ds(at, 256), :] = jnp.where(rows == column, 1.0, 0.0).astype(BF)

    @pl.loop(0, SW // 128)
    def _(b):
        rows = pl.ds(pl.multiple_of(b * 128, 128), 128)
        strips = pl.ds(b * (128 // KB), 128 // KB)
        real = jnp.dot(
            data_v[0, strips].reshape(128, NS), sel[...], preferred_element_type=F32
        )
        imag = jnp.dot(
            data_v[1, strips].reshape(128, NS), sel[...], preferred_element_type=F32
        )
        left_a[rows, :RK] = real.astype(BF)
        left_a[rows, RK:] = (-imag).astype(BF)
        left_b[rows, :RK] = imag.astype(BF)
        left_b[rows, RK:] = real.astype(BF)

    left_t[...] = left_a[...].T

    loads[1].wait()
    loads[2].wait()
    spectrum = lax.dot_general(
        table_v[...], traces_v[...], (((1,), (1,)), ((), ())), preferred_element_type=F32
    ).astype(BF)

    blocks = GROUP // BLOCK

    def prepare(g):
        @pl.loop(0, blocks)
        def _(b):
            lanes = pl.ds(pl.multiple_of(b * BLOCK, BLOCK), BLOCK)
            row = (g * blocks + b) * 2
            recv = jnp.concatenate([recv_v[pl.ds(row, 1), :], recv_v[pl.ds(row + 1, 1), :]], axis=1)
            shot = jnp.concatenate([shot_v[pl.ds(row, 1), :], shot_v[pl.ds(row + 1, 1), :]], axis=1)
            for c in range(NS // 256):
                rows = lax.broadcasted_iota(jnp.int32, (256, BLOCK), 0) + c * 256
                hot[c * 256 : (c + 1) * 256, lanes] = jnp.where(rows == recv, 1.0, 0.0).astype(BF)
            mine = lax.broadcasted_iota(jnp.int32, (SW, BLOCK), 0) + reader * SW
            mine = jnp.where(mine == shot, 1.0, 0.0).astype(BF)
            lsel[:, lanes] = jnp.dot(left_t[...], mine, preferred_element_type=F32)

    def pick(c):
        @pl.loop(0, blocks)
        def _(b):
            lanes = pl.ds(pl.multiple_of(b * BLOCK, BLOCK), BLOCK)
            got = jnp.dot(
                panels[c].reshape(2 * RK, W),
                hot[c * W : (c + 1) * W, lanes],
                preferred_element_type=F32,
            )
            lefts = lsel[:, lanes]
            real = jnp.sum(lefts * got, axis=0, keepdims=True)
            imag = jnp.sum(lefts[:RK] * got[RK:] - lefts[RK:] * got[:RK], axis=0, keepdims=True)
            if c == 0:
                acc[0:1, lanes] = real
                acc[1:2, lanes] = imag
            else:
                acc[0:1, lanes] += real
                acc[1:2, lanes] += imag

    def keep(g):
        for i in range(GROUP // LANES):
            value = acc[0:2, i * LANES : (i + 1) * LANES].astype(BF).astype(F32)
            picks[g * (GROUP // LANES) + i, 0:2, :] = value

    def multiply(c):
        @pl.loop(0, SW // 128)
        def _(b):
            rows = pl.ds(pl.multiple_of(b * 128, 128), 128)
            right = panels[c].reshape(2 * RK, W)
            stage[c, 0, rows, :] = jnp.dot(
                left_a[rows, :], right, preferred_element_type=F32
            ).astype(BF)
            stage[c, 1, rows, :] = jnp.dot(
                left_b[rows, :], right, preferred_element_type=F32
            ).astype(BF)

        out_copy(c).start()

    def out_copy(c):
        return pltpu.make_async_copy(
            stage.at[c], out_hbm.at[0, :, :, pl.ds(c * W, W)], out_sem.at[c]
        )

    picks[...] = jnp.zeros_like(picks)
    prepare(0)
    for c in range(CHUNKS):
        for n, (dp, dr) in enumerate(offsets):
            sender = lax.rem(pan + PAN - dp, PAN) * REP + lax.rem(rep + REP - dr, REP)
            panel_copy(n, c, sender).wait_recv()
        pick(c)
        if c < CHUNKS - 1:
            multiply(c)
    keep(0)

    @pl.loop(1, (NF * R * TL) // GROUP)
    def _(g):
        prepare(g)
        for c in range(CHUNKS):
            pick(c)
        keep(g)

    def pick_copy(k, target, slot):
        return pltpu.make_async_remote_copy(
            src_ref=picks.at[lax.div(target, PB)],
            dst_ref=arrived.at[slot],
            send_sem=pick_send.at[k],
            recv_sem=pick_recv.at[k],
            device_id=place(target),
            device_id_type=MESH,
        )

    @pl.loop(1, N)
    def _(k):
        pick_copy(k, lax.rem(me + k, N), me).start()

    arrived[me] = picks[lax.div(me, PB)]
    multiply(CHUNKS - 1)

    @pl.loop(1, N)
    def _(k):
        pick_copy(k, lax.rem(me + k, N), lax.rem(me + N - k, N)).wait_recv()

    for j in range(NF):
        total = arrived[j * R]
        for r in range(1, R):
            total = total + arrived[j * R + r]
        tidy[j : j + 1, :] = total[0:1]
        tidy[NF + j : NF + j + 1, :] = total[1:2]
    part = lax.rem(me, PB)
    value = tidy[:, :TL]
    for h in range(1, PB):
        value = jnp.where(part == h, tidy[:, h * TL : (h + 1) * TL], value)
    prim_v[...] = spectrum.astype(F32)[: 2 * NF] - value

    @pl.loop(1, N)
    def _(k):
        pick_copy(k, lax.rem(me + k, N), me).wait_send()

    for c in range(CHUNKS):
        for n in range(R - 1):
            panel_copy(n, c, reader).wait_send()
        out_copy(c).wait()


def local(traces, data, trace_shot, trace_recv, aper_panel, aper_order, aper_count):
    NF = lax.axis_size("freq") * data.shape[0]
    PAN, REP = lax.axis_size("pan"), lax.axis_size("rep")
    R = PAN * REP
    N = NF * R
    SW, NS = data.shape[2], data.shape[3]
    TL, NT = traces.shape
    total = trace_shot.shape[0]
    GROUP = min(total, 1024)
    W = NS // CHUNKS
    RK = R * KB
    table = jnp.asarray(spectral_table(NT, NF, FBIN0, FSTEP))
    sizes = (NF, PAN, REP, SW, NS, TL, GROUP)
    vmem = pl.BlockSpec(memory_space=pltpu.VMEM)
    smem = pl.BlockSpec(memory_space=pltpu.SMEM)
    hbm = pl.BlockSpec(memory_space=pl.ANY)
    multiples, primaries = pl.pallas_call(
        functools.partial(kernel, sizes),
        out_shape=(
            jax.ShapeDtypeStruct((1, 2, SW, NS), BF),
            jax.ShapeDtypeStruct((2 * NF, TL), F32),
        ),
        in_specs=[hbm, hbm, hbm, smem, smem, smem, vmem, vmem],
        out_specs=(hbm, vmem),
        scratch_shapes=[
            pltpu.VMEM((2, SW // KB, KB, NS), BF),
            pltpu.VMEM((TL, NT), BF),
            pltpu.VMEM(table.shape, BF),
            pltpu.VMEM((R - 1, CHUNKS, 2, KB, W), BF),
            pltpu.VMEM((CHUNKS, 2, R, KB, W), BF),
            pltpu.VMEM((NS, RK), BF),
            pltpu.VMEM((SW, 2 * RK), BF),
            pltpu.VMEM((SW, 2 * RK), BF),
            pltpu.VMEM((2 * RK, SW), BF),
            pltpu.VMEM((NS, GROUP), BF),
            pltpu.VMEM((2 * RK, GROUP), F32),
            pltpu.VMEM((8, GROUP), F32),
            pltpu.VMEM((total // LANES, 8, LANES), F32),
            pltpu.VMEM((N, 8, LANES), F32),
            pltpu.VMEM((2 * NF, LANES), F32),
            pltpu.VMEM((CHUNKS, 2, SW, W), BF),
            pltpu.SemaphoreType.DMA((3,)),
            pltpu.SemaphoreType.DMA((R - 1, CHUNKS)),
            pltpu.SemaphoreType.DMA((R - 1, CHUNKS)),
            pltpu.SemaphoreType.DMA((N,)),
            pltpu.SemaphoreType.DMA((N,)),
            pltpu.SemaphoreType.DMA((CHUNKS,)),
        ],
        compiler_params=pltpu.CompilerParams(
            collective_id=0, has_side_effects=True, vmem_limit_bytes=48 * 1024 * 1024
        ),
    )(
        data.reshape(1, 2, SW // KB, KB, NS),
        traces,
        table,
        aper_panel,
        aper_order,
        aper_count,
        trace_shot.reshape(-1, LANES),
        trace_recv.reshape(-1, LANES),
    )
    return multiples, jnp.transpose(primaries.reshape(2, NF, TL), (2, 0, 1))


def solution(mesh):
    in_specs = (
        P(("parts", "freq", "pan", "rep"), None),
        P(("parts", "freq"), None, ("pan", "rep"), None),
        P("parts"),
        P("parts"),
        P("parts", None),
        P("parts", None),
        P("parts"),
    )
    out_specs = (
        P(("parts", "freq"), None, ("pan", "rep"), None),
        P(("parts", "freq", "pan", "rep"), None, None),
    )
    return jax.shard_map(local, mesh=mesh, in_specs=in_specs, out_specs=out_specs, check_vma=False)
```

time: 112 us -> 33.7 us (0.30); the launches traced: 109 us -> 33.4 us
  local copies, waits for them, and re-layouts: 59.9 us -> 7.94 us
  Pallas kernels: 0 us -> 24.8 us
  starting transfers between devices: 21.9 us -> 0 us
  other arithmetic: 17.5 us -> 0 us
  waiting for transfers between devices: 6.07 us -> 0 us
  matrix products: 3.15 us -> 0 us
    pallas_call x0 -> x1, Pallas kernels: none -> 24.8 us  [local(): pl.pallas_call(functools.partial(kernel, sizes), out_shape=(jax.ShapeDtyp...]
    all_to_all x5 -> x0, starting transfers between devices: 21.9 us -> none  [the longest x1 6.32 us: local(): lax.all_to_all(buckets, 'freq', split_axis=3, concat_axis=1, tiled=True)]
    gather x4 -> x0, local copies, waits for them, and re-layouts: 20.2 us -> none  [the longest x1 13.4 us: local(): multiples[:, :, slot_shot, slot_recv]]
    scatter x3 -> x0, local copies, waits for them, and re-layouts: 13.1 us -> none  [the longest x1 4.46 us: local(): jnp.zeros((slot_total,), jnp.int32).at[target].set(trace_recv, mode='drop')]
    another operation x5 -> x0, other arithmetic: 8.51 us -> none  [the longest x2 6.36 us: local(): multiples = jnp.stack([real_part, imag_part], axis=1).astype(jnp.bfloat16)]
    another operation x1 -> x0, local copies, waits for them, and re-layouts: 8.42 us -> none  [local(): multiples = jnp.stack([real_part, imag_part], axis=1).astype(jnp.bfloat16)]
    unnamed x18 -> x16, local copies, waits for them, and re-layouts: 15.5 us -> 7.94 us
    all_to_all x5 -> x0, waiting for transfers between devices: 6.07 us -> none  [the longest x1 5.57 us: local(): lax.all_to_all(difference, 'freq', split_axis=1, concat_axis=4, tiled=True)]
  transfers between devices with their start and end apart: 5 -> 0, of which waited for: 2 -> 0; matrix products, arithmetic and copies ran while one was open for 63% -> 0% of each run, Pallas kernels for 0% -> 0%
where the time goes in v1:
time: 33.7 us; the launch traced here: 33.4 us
  Pallas kernels  24.8 us (74%)
  local copies, waits for them, and re-layouts  7.94 us (24%)
  between operations  0.66 us (2%)
    pallas_call x1, Pallas kernels, local(): pl.pallas_call(functools.partial(kernel, sizes), out_shape=(jax.ShapeDtyp...  24.8 us
    unnamed x16, local copies, waits for them, and re-layouts  7.94 us

profile of v1, /device:TPU:0, one launch (start us, length us, event | category | flops | bytes accessed | tf_op | source)
XLA Modules:
  0.0 33.4 jit_solution(13536148240808764162)
XLA Ops:
  0.6 0.0 copy-start
  0.6 1.0 %copy-done = bf16[64,4096]{1,0:T(8,128)(2,1)S(1)} copy-done((bf16[64,4096]{1,0:T(8,128)(2,1)S(1)}, bf16[64,4096]{1,0:T(8,128)(2,1)}, u32[]{:S(2)}) %copy-start) | copy-done | bytes 524312
  1.7 0.0 copy-start.1
  1.7 0.9 %copy-done.1 = bf16[16,4096]{1,0:T(8,128)(2,1)S(1)} copy-done((bf16[16,4096]{1,0:T(8,128)(2,1)S(1)}, bf16[16,4096]{1,0:T(8,128)(2,1)}, u32[]{:S(2)}) %copy-start.1) | copy-done | bytes 131096
  2.6 0.0 copy-start.2
  2.6 0.7 %copy-done.2 = s32[1024]{0:T(1024)S(1)} copy-done((s32[1024]{0:T(1024)S(1)}, s32[1024]{0:T(1024)}, u32[]{:S(2)}) %copy-start.2) | copy-done | bytes 4120
  3.3 0.0 copy-start.3
  3.3 0.7 %copy-done.3 = s32[1024]{0:T(1024)S(1)} copy-done((s32[1024]{0:T(1024)S(1)}, s32[1024]{0:T(1024)}, u32[]{:S(2)}) %copy-start.3) | copy-done | bytes 4120
  4.0 0.0 copy-start.4
  4.0 0.7 %copy-done.4 = s32[4,4]{1,0:T(4,128)S(1)} copy-done((s32[4,4]{1,0:T(4,128)S(1)}, s32[4,4]{1,0:T(4,128)}, u32[]{:S(2)}) %copy-start.4) | copy-done | bytes 88
  4.6 0.0 copy-start.5
  4.6 0.7 %copy-done.5 = s32[4,4]{1,0:T(4,128)S(1)} copy-done((s32[4,4]{1,0:T(4,128)S(1)}, s32[4,4]{1,0:T(4,128)}, u32[]{:S(2)}) %copy-start.5) | copy-done | bytes 88
  5.3 0.0 copy-start.6
  5.3 0.7 %copy-done.6 = s32[4]{0:T(128)S(1)} copy-done((s32[4]{0:T(128)S(1)}, s32[4]{0:T(128)}, u32[]{:S(2)}) %copy-start.6) | copy-done | bytes 40
  6.0 24.8 %shard_map.95 = (bf16[1,2,512,2048]{3,2,1,0:T(8,128)(2,1)S(1)}, f32[8,64]{1,0:T(8,128)S(1)}) custom-call(bf16[1,2,16,32,2048]{4,3,2,1,0:T(8,128)(2,1)} %bitcast.9, bf16[64,4096]{1,0:T(8,128)(2,1)S(1)} %copy-done, bf16[16,4096]{1,0:T(8,128)(2,1)S(1)} %copy-done.1, s32[4,4]{1,0:T(4,128)S(1)} %copy-done.4, s32[4,4]{1,0:T(4,128)S(1)} %copy-done.5, ...), custom_call_target="tpu_custom_call" | custom-call | tf_op jit(solution)/shard_map/pallas_call | solution.py:276
  30.8 2.0 %copy.12 = bf16[1,2,512,2048]{3,2,1,0:T(8,128)(2,1)} copy(bf16[1,2,512,2048]{3,2,1,0:T(8,128)(2,1)S(1)} %get-tuple-element.8) | data formatting | bytes 8388608
  32.8 0.6 %copy.13 = f32[64,2,4]{0,2,1:T(4,128)} copy(f32[64,2,4]{0,2,1:T(4,128)S(1)} %bitcast.6) | data formatting | bytes 4096
Async XLA Ops:
  0.6 1.0 %copy-start = (bf16[64,4096]{1,0:T(8,128)(2,1)S(1)}, bf16[64,4096]{1,0:T(8,128)(2,1)}, u32[]{:S(2)}) copy-start(bf16[64,4096]{1,0:T(8,128)(2,1)} %traces_hbm.1) | copy-start | bytes 1572868
  1.7 0.9 %copy-start.1 = (bf16[16,4096]{1,0:T(8,128)(2,1)S(1)}, bf16[16,4096]{1,0:T(8,128)(2,1)}, u32[]{:S(2)}) copy-start(bf16[16,4096]{1,0:T(8,128)(2,1)} %constant.2.clone.table_hbm) | copy-start | bytes 393220
  2.6 0.7 %copy-start.2 = (s32[1024]{0:T(1024)S(1)}, s32[1024]{0:T(1024)}, u32[]{:S(2)}) copy-start(s32[1024]{0:T(1024)} %param.10) | copy-start | bytes 12292
  3.3 0.7 %copy-start.3 = (s32[1024]{0:T(1024)S(1)}, s32[1024]{0:T(1024)}, u32[]{:S(2)}) copy-start(s32[1024]{0:T(1024)} %param.11) | copy-start | bytes 12292
  4.0 0.7 %copy-start.4 = (s32[4,4]{1,0:T(4,128)S(1)}, s32[4,4]{1,0:T(4,128)}, u32[]{:S(2)}) copy-start(s32[4,4]{1,0:T(4,128)} %panel_s.1) | copy-start | bytes 196
  4.6 0.7 %copy-start.5 = (s32[4,4]{1,0:T(4,128)S(1)}, s32[4,4]{1,0:T(4,128)}, u32[]{:S(2)}) copy-start(s32[4,4]{1,0:T(4,128)} %order_s.1) | copy-start | bytes 196
  5.3 0.7 %copy-start.6 = (s32[4]{0:T(128)S(1)}, s32[4]{0:T(128)}, u32[]{:S(2)}) copy-start(s32[4]{0:T(128)} %count_s.1) | copy-start | bytes 52

commit v2 on v1

--- a/solution.py
+++ b/solution.py
@@ -34,9 +34,9 @@
 
 def kernel(
     sizes,
-    data_hbm, traces_hbm, table_hbm, panel_s, order_s, count_s, shot_v, recv_v,
+    data_hbm, traces_hbm, table_hbm, panel_hbm, order_hbm, count_hbm, shot_hbm, recv_hbm,
     out_hbm, prim_v,
-    data_v, traces_v, table_v, send, panels, sel, left_a, left_b, left_t, hot, lsel, acc, picks,
+    panel_s, order_s, count_s, shot_v, recv_v, data_v, traces_v, table_v, send, panels, sel, left_a, left_b, left_t, hot, lsel, acc, picks,
     arrived, tidy, stage,
     load_sem, send_sem, recv_sem, pick_send, pick_recv, out_sem,
 ):
@@ -55,9 +55,14 @@
         return {"freq": lax.div(s, R), "pan": lax.div(r, REP), "rep": lax.rem(r, REP)}
 
     loads = [
-        pltpu.make_async_copy(data_hbm.at[0], data_v, load_sem.at[0]),
-        pltpu.make_async_copy(traces_hbm, traces_v, load_sem.at[1]),
-        pltpu.make_async_copy(table_hbm, table_v, load_sem.at[2]),
+        pltpu.make_async_copy(panel_hbm, panel_s, load_sem.at[0]),
+        pltpu.make_async_copy(data_hbm.at[0], data_v, load_sem.at[1]),
+        pltpu.make_async_copy(order_hbm, order_s, load_sem.at[2]),
+        pltpu.make_async_copy(count_hbm, count_s, load_sem.at[3]),
+        pltpu.make_async_copy(shot_hbm, shot_v, load_sem.at[4]),
+        pltpu.make_async_copy(recv_hbm, recv_v, load_sem.at[5]),
+        pltpu.make_async_copy(traces_hbm, traces_v, load_sem.at[6]),
+        pltpu.make_async_copy(table_hbm, table_v, load_sem.at[7]),
     ]
     for copy in loads:
         copy.start()
@@ -71,6 +76,7 @@
         )
 
     loads[0].wait()
+    loads[1].wait()
     offsets = [(dp, dr) for dp in range(PAN) for dr in range(REP) if (dp, dr) != (0, 0)]
     offsets = [o for o in offsets if o[0]] + [o for o in offsets if not o[0]]
 
@@ -98,6 +104,8 @@
     for c in range(CHUNKS):
         panels[c, :, reader] = data_v[:, p, :, c * W : (c + 1) * W]
 
+    loads[2].wait()
+    loads[3].wait()
     lane = lax.broadcasted_iota(jnp.int32, (1, RK), 1)
     column = jnp.full((1, RK), -1, jnp.int32)
     for q in range(R):
@@ -131,8 +139,8 @@
 
     left_t[...] = left_a[...].T
 
-    loads[1].wait()
-    loads[2].wait()
+    for copy in loads[4:]:
+        copy.wait()
     spectrum = lax.dot_general(
         table_v[...], traces_v[...], (((1,), (1,)), ((), ())), preferred_element_type=F32
     ).astype(BF)
@@ -271,17 +279,22 @@
     table = jnp.asarray(spectral_table(NT, NF, FBIN0, FSTEP))
     sizes = (NF, PAN, REP, SW, NS, TL, GROUP)
     vmem = pl.BlockSpec(memory_space=pltpu.VMEM)
-    smem = pl.BlockSpec(memory_space=pltpu.SMEM)
-    hbm = pl.BlockSpec(memory_space=pl.ANY)
+    hbm = pl.BlockSpec(memory_space=pltpu.HBM)
+    anywhere = pl.BlockSpec(memory_space=pl.ANY)
     multiples, primaries = pl.pallas_call(
         functools.partial(kernel, sizes),
         out_shape=(
             jax.ShapeDtypeStruct((1, 2, SW, NS), BF),
             jax.ShapeDtypeStruct((2 * NF, TL), F32),
         ),
-        in_specs=[hbm, hbm, hbm, smem, smem, smem, vmem, vmem],
-        out_specs=(hbm, vmem),
+        in_specs=[hbm] * 8,
+        out_specs=(anywhere, vmem),
         scratch_shapes=[
+            pltpu.SMEM((R, R), jnp.int32),
+            pltpu.SMEM((R, R), jnp.int32),
+            pltpu.SMEM((R,), jnp.int32),
+            pltpu.VMEM((total // LANES, LANES), jnp.int32),
+            pltpu.VMEM((total // LANES, LANES), jnp.int32),
             pltpu.VMEM((2, SW // KB, KB, NS), BF),
             pltpu.VMEM((TL, NT), BF),
             pltpu.VMEM(table.shape, BF),
@@ -298,7 +311,7 @@
             pltpu.VMEM((N, 8, LANES), F32),
             pltpu.VMEM((2 * NF, LANES), F32),
             pltpu.VMEM((CHUNKS, 2, SW, W), BF),
-            pltpu.SemaphoreType.DMA((3,)),
+            pltpu.SemaphoreType.DMA((8,)),
             pltpu.SemaphoreType.DMA((R - 1, CHUNKS)),
             pltpu.SemaphoreType.DMA((R - 1, CHUNKS)),
             pltpu.SemaphoreType.DMA((N,)),
@@ -309,14 +322,19 @@
             collective_id=0, has_side_effects=True, vmem_limit_bytes=48 * 1024 * 1024
         ),
     )(
-        data.reshape(1, 2, SW // KB, KB, NS),
-        traces,
-        table,
-        aper_panel,
-        aper_order,
-        aper_count,
-        trace_shot.reshape(-1, LANES),
-        trace_recv.reshape(-1, LANES),
+        *(
+            pltpu.with_memory_space_constraint(operand, pltpu.HBM)
+            for operand in (
+                data.reshape(1, 2, SW // KB, KB, NS),
+                traces,
+                table,
+                aper_panel,
+                aper_order,
+                aper_count,
+                trace_shot.reshape(-1, LANES),
+                trace_recv.reshape(-1, LANES),
+            )
+        )
     )
     return multiples, jnp.transpose(primaries.reshape(2, NF, TL), (2, 0, 1))
 

time: 33.7 us -> 27.6 us (0.82)
  local copies, waits for them, and re-layouts: 7.94 us -> 2.61 us
  Pallas kernels: 24.8 us -> 24.2 us
    unnamed x16 -> x2, local copies, waits for them, and re-layouts: 7.94 us -> 2.61 us
    pallas_call x1, Pallas kernels: 24.8 us -> 24.2 us  [local(): pl.pallas_call(functools.partial(kernel, sizes), out_shape=(jax.ShapeDtyp...]
where the time goes in v2:
time: 27.6 us; the launch traced here: 27.4 us
  Pallas kernels  24.2 us (88%)
  local copies, waits for them, and re-layouts  2.61 us (9%)
  between operations  0.64 us (2%)
    pallas_call x1, Pallas kernels, local(): pl.pallas_call(functools.partial(kernel, sizes), out_shape=(jax.ShapeDtyp...  24.2 us
    unnamed x2, local copies, waits for them, and re-layouts  2.61 us

profile of v2, /device:TPU:0, one launch (start us, length us, event | category | flops | bytes accessed | tf_op | source)
XLA Modules:
  0.0 27.4 jit_solution(17153282896024939295)
XLA Ops:
  0.6 24.2 %shard_map.95 = (bf16[1,2,512,2048]{3,2,1,0:T(8,128)(2,1)S(1)}, f32[8,64]{1,0:T(8,128)S(1)}) custom-call(bf16[1,2,16,32,2048]{4,3,2,1,0:T(8,128)(2,1)} %bitcast.7, bf16[64,4096]{1,0:T(8,128)(2,1)} %traces_hbm.1, bf16[16,4096]{1,0:T(8,128)(2,1)} %constant.2.clone.table_hbm, s32[4,4]{1,0:T(4,128)} %panel_hbm.1, s32[4,4]{1,0:T(4,128)} %order_hbm.1, ...), custom_call_target="tpu_custom_call" | custom-call | tf_op jit(solution)/shard_map/pallas_call | solution.py:284
  24.8 2.0 %copy.12 = bf16[1,2,512,2048]{3,2,1,0:T(8,128)(2,1)} copy(bf16[1,2,512,2048]{3,2,1,0:T(8,128)(2,1)S(1)} %get-tuple-element.8) | data formatting | bytes 8388608
  26.8 0.6 %copy.13 = f32[64,2,4]{0,2,1:T(4,128)} copy(f32[64,2,4]{0,2,1:T(4,128)S(1)} %bitcast.6) | data formatting | bytes 4096

commit v3 on v2

--- a/solution.py
+++ b/solution.py
@@ -38,7 +38,7 @@
     out_hbm, prim_v,
     panel_s, order_s, count_s, shot_v, recv_v, data_v, traces_v, table_v, send, panels, sel, left_a, left_b, left_t, hot, lsel, acc, picks,
     arrived, tidy, stage,
-    load_sem, send_sem, recv_sem, pick_send, pick_recv, out_sem,
+    load_sem, send_sem, recv_sem, pick_send, pick_recv, out_sem, up_sem, down_sem, all_sem,
 ):
     NF, PAN, REP, SW, NS, TL, GROUP = sizes
     R = PAN * REP
@@ -50,9 +50,43 @@
     reader = pan * REP + rep
     me = freq * R + reader
 
-    def place(s):
-        r = lax.rem(s, R)
-        return {"freq": lax.div(s, R), "pan": lax.div(r, REP), "rep": lax.rem(r, REP)}
+    def turn(at, step, size):
+        return at if isinstance(step, int) and step == 0 else lax.rem(at + step, size)
+
+    pans = [turn(pan, k, PAN) for k in range(PAN)]
+    reps = [turn(rep, k, REP) for k in range(REP)]
+    back_pans = [turn(pan, PAN - k, PAN) if k else pan for k in range(PAN)]
+    back_reps = [turn(rep, REP - k, REP) if k else rep for k in range(REP)]
+
+    def each_peer(act):
+        def band(k):
+            there = turn(freq, k, NF)
+            back = freq if isinstance(k, int) and k == 0 else lax.rem(freq + NF - k, NF)
+            for dp in range(PAN):
+                for dr in range(REP):
+                    if isinstance(k, int) and (k, dp, dr) == (0, 0, 0):
+                        continue
+                    act(
+                        k * R + dp * REP + dr,
+                        (there, pans[dp], reps[dr]),
+                        (back, back_pans[dp], back_reps[dr]),
+                    )
+
+        band(0)
+        if N <= 32:
+            for k in range(1, NF):
+                band(k)
+        else:
+            pl.loop(1, NF)(band)
+
+    def place(spot):
+        return {"freq": spot[0], "pan": spot[1], "rep": spot[2]}
+
+    def number(spot):
+        return spot[0] * R + spot[1] * REP + spot[2]
+
+    def lane_block(spot):
+        return spot[0] * PAN + spot[1] if REP == PB else lax.div(number(spot), PB)
 
     loads = [
         pltpu.make_async_copy(panel_hbm, panel_s, load_sem.at[0]),
@@ -69,22 +103,41 @@
 
     barrier = pltpu.get_barrier_semaphore()
 
-    @pl.loop(1, N)
-    def _(k):
-        pl.semaphore_signal(
-            barrier, inc=1, device_id=place(lax.rem(me + k, N)), device_id_type=MESH
-        )
+    offsets = [(dp, dr) for dp in range(PAN) for dr in range(REP) if (dp, dr) != (0, 0)]
+    offsets = [o for o in offsets if o[0]] + [o for o in offsets if not o[0]]
+    gate = reader == 0
+    above, below = gate & (freq > 0), gate & (freq < NF - 1)
+
+    def tell(sem, **where):
+        pl.semaphore_signal(sem, inc=1, device_id=where, device_id_type=MESH)
+
+    for dp, dr in offsets:
+        tell(barrier, pan=pans[dp], rep=reps[dr])
+    pl.when(above)(lambda: tell(barrier, freq=freq - 1))
+    pl.when(below)(lambda: tell(barrier, freq=freq + 1))
+
+    def send_up():
+        tell(up_sem, freq=freq + 1)
+
+    def send_down():
+        tell(down_sem, freq=freq - 1)
+
+    def pass_up():
+        pl.semaphore_wait(up_sem, 1)
+        send_up()
+
+    def pass_down():
+        pl.semaphore_wait(down_sem, 1)
+        send_down()
 
     loads[0].wait()
     loads[1].wait()
-    offsets = [(dp, dr) for dp in range(PAN) for dr in range(REP) if (dp, dr) != (0, 0)]
-    offsets = [o for o in offsets if o[0]] + [o for o in offsets if not o[0]]
-
     for n, (dp, dr) in enumerate(offsets):
-        p = panel_s[lax.rem(pan + dp, PAN) * REP + lax.rem(rep + dr, REP), reader]
+        p = panel_s[pans[dp] * REP + reps[dr], reader]
         for c in range(CHUNKS):
             send[n, c] = data_v[:, p, :, c * W : (c + 1) * W]
-    pl.semaphore_wait(barrier, N - 1)
+    bands_beside = lax.div(freq + NF - 1, NF) + 1 - lax.div(freq + 1, NF)
+    pl.semaphore_wait(barrier, R - 1 + (1 - lax.div(reader + R - 1, R)) * bands_beside)
 
     def panel_copy(n, c, slot):
         dp, dr = offsets[n]
@@ -93,13 +146,15 @@
             dst_ref=panels.at[c, :, slot],
             send_sem=send_sem.at[n, c],
             recv_sem=recv_sem.at[n, c],
-            device_id={"pan": lax.rem(pan + dp, PAN), "rep": lax.rem(rep + dr, REP)},
+            device_id={"pan": pans[dp], "rep": reps[dr]},
             device_id_type=MESH,
         )
 
     for c in range(CHUNKS):
         for n in range(R - 1):
             panel_copy(n, c, reader).start()
+    pl.when(gate & (freq == 0))(send_up)
+    pl.when(gate & (freq == NF - 1))(send_down)
     p = panel_s[reader, reader]
     for c in range(CHUNKS):
         panels[c, :, reader] = data_v[:, p, :, c * W : (c + 1) * W]
@@ -144,6 +199,9 @@
     spectrum = lax.dot_general(
         table_v[...], traces_v[...], (((1,), (1,)), ((), ())), preferred_element_type=F32
     ).astype(BF)
+
+    pl.when(gate & (freq == 1))(pass_up)
+    pl.when(gate & (freq == NF - 2))(pass_down)
 
     blocks = GROUP // BLOCK
 
@@ -206,14 +264,26 @@
 
     picks[...] = jnp.zeros_like(picks)
     prepare(0)
+    pl.when(gate & (freq >= 2) & (freq <= NF - 2))(pass_up)
+    pl.when(gate & (freq >= 1) & (freq <= NF - 3))(pass_down)
     for c in range(CHUNKS):
         for n, (dp, dr) in enumerate(offsets):
-            sender = lax.rem(pan + PAN - dp, PAN) * REP + lax.rem(rep + REP - dr, REP)
+            sender = back_pans[dp] * REP + back_reps[dr]
             panel_copy(n, c, sender).wait_recv()
         pick(c)
         if c < CHUNKS - 1:
             multiply(c)
+        if c == 1:
+
+            @pl.when(gate)
+            def _():
+                pl.when(freq == NF - 1)(lambda: pl.semaphore_wait(up_sem, 1))
+                pl.when(freq == 0)(lambda: pl.semaphore_wait(down_sem, 1))
+                for dp, dr in offsets:
+                    tell(all_sem, pan=pans[dp], rep=reps[dr])
+
     keep(0)
+    pl.when(reader > 0)(lambda: pl.semaphore_wait(all_sem, 1))
 
     @pl.loop(1, (NF * R * TL) // GROUP)
     def _(g):
@@ -224,7 +294,7 @@
 
     def pick_copy(k, target, slot):
         return pltpu.make_async_remote_copy(
-            src_ref=picks.at[lax.div(target, PB)],
+            src_ref=picks.at[lane_block(target)],
             dst_ref=arrived.at[slot],
             send_sem=pick_send.at[k],
             recv_sem=pick_recv.at[k],
@@ -232,16 +302,10 @@
             device_id_type=MESH,
         )
 
-    @pl.loop(1, N)
-    def _(k):
-        pick_copy(k, lax.rem(me + k, N), me).start()
-
-    arrived[me] = picks[lax.div(me, PB)]
+    each_peer(lambda k, target, source: pick_copy(k, target, me).start())
+    arrived[me] = picks[lane_block((freq, pan, rep))]
     multiply(CHUNKS - 1)
-
-    @pl.loop(1, N)
-    def _(k):
-        pick_copy(k, lax.rem(me + k, N), lax.rem(me + N - k, N)).wait_recv()
+    each_peer(lambda k, target, source: pick_copy(k, target, number(source)).wait_recv())
 
     for j in range(NF):
         total = arrived[j * R]
@@ -249,20 +313,37 @@
             total = total + arrived[j * R + r]
         tidy[j : j + 1, :] = total[0:1]
         tidy[NF + j : NF + j + 1, :] = total[1:2]
-    part = lax.rem(me, PB)
+    part = rep if REP == PB else lax.rem(me, PB)
     value = tidy[:, :TL]
     for h in range(1, PB):
         value = jnp.where(part == h, tidy[:, h * TL : (h + 1) * TL], value)
     prim_v[...] = spectrum.astype(F32)[: 2 * NF] - value
 
-    @pl.loop(1, N)
-    def _(k):
-        pick_copy(k, lax.rem(me + k, N), me).wait_send()
-
+    each_peer(lambda k, target, source: pick_copy(k, target, me).wait_send())
     for c in range(CHUNKS):
         for n in range(R - 1):
             panel_copy(n, c, reader).wait_send()
         out_copy(c).wait()
+
+
+def finish(multiples, primaries, multiples_out, primaries_out, sems):
+    half = multiples.shape[2] // 2
+    copies = []
+    for part in range(2):
+        for h in range(2):
+            where = (0, part, slice(h * half, (h + 1) * half))
+            copies.append(
+                pltpu.make_async_copy(
+                    multiples.at[where], multiples_out.at[where], sems.at[2 * part + h]
+                )
+            )
+    for copy in copies:
+        copy.start()
+    count = primaries_out.shape[1]
+    primaries_out[0] = primaries[:count]
+    primaries_out[1] = primaries[count:]
+    for copy in copies:
+        copy.wait()
 
 
 def local(traces, data, trace_shot, trace_recv, aper_panel, aper_order, aper_count):
@@ -317,6 +398,9 @@
             pltpu.SemaphoreType.DMA((N,)),
             pltpu.SemaphoreType.DMA((N,)),
             pltpu.SemaphoreType.DMA((CHUNKS,)),
+            pltpu.SemaphoreType.REGULAR,
+            pltpu.SemaphoreType.REGULAR,
+            pltpu.SemaphoreType.REGULAR,
         ],
         compiler_params=pltpu.CompilerParams(
             collective_id=0, has_side_effects=True, vmem_limit_bytes=48 * 1024 * 1024
@@ -336,7 +420,17 @@
             )
         )
     )
-    return multiples, jnp.transpose(primaries.reshape(2, NF, TL), (2, 0, 1))
+    multiples, primaries = pl.pallas_call(
+        finish,
+        out_shape=(
+            jax.ShapeDtypeStruct((1, 2, SW, NS), BF),
+            jax.ShapeDtypeStruct((2, NF, TL), F32),
+        ),
+        in_specs=[anywhere, vmem],
+        out_specs=(hbm, vmem),
+        scratch_shapes=[pltpu.SemaphoreType.DMA((4,))],
+    )(multiples, primaries)
+    return multiples, jnp.transpose(primaries, (2, 0, 1))
 
 
 def solution(mesh):

time: 27.6 us -> 157 us (5.69)
  Pallas kernels: 24.2 us -> 153 us
    pallas_call x0 -> x1, Pallas kernels: none -> 129 us  [local(): pl.pallas_call(finish, out_shape=(jax.ShapeDtypeStruct((1, 2, SW, NS), BF...]
where the time goes in v3:
time: 157 us
  Pallas kernels  153 us (97%)
  local copies, waits for them, and re-layouts  2.52 us (2%)
    pallas_call x1, Pallas kernels, local(): pl.pallas_call(finish, out_shape=(jax.ShapeDtypeStruct((1, 2, SW, NS), BF...  129 us
    pallas_call x1, Pallas kernels, local(): pl.pallas_call(functools.partial(kernel, sizes), out_shape=(jax.ShapeDtyp...  24 us

profile of v3, /device:TPU:0, one launch (start us, length us, event | category | flops | bytes accessed | tf_op | source)
XLA Modules:
  0.0 156.6 jit_solution(11470682415671597845)
XLA Ops:
  0.6 24.0 %shard_map.95 = (bf16[1,2,512,2048]{3,2,1,0:T(8,128)(2,1)S(1)}, f32[8,64]{1,0:T(8,128)S(1)}) custom-call(bf16[1,2,16,32,2048]{4,3,2,1,0:T(8,128)(2,1)} %bitcast.4, bf16[64,4096]{1,0:T(8,128)(2,1)} %traces_hbm.1, bf16[16,4096]{1,0:T(8,128)(2,1)} %constant.2.clone.table_hbm, s32[4,4]{1,0:T(4,128)} %panel_hbm.1, s32[4,4]{1,0:T(4,128)} %order_hbm.1, ...), custom_call_target="tpu_custom_call" | custom-call | tf_op jit(solution)/shard_map/pallas_call | solution.py:365
  24.7 0.0 copy-start
  24.7 1.9 %copy-done = bf16[1,2,512,2048]{3,2,1,0:T(8,128)(2,1)} copy-done((bf16[1,2,512,2048]{3,2,1,0:T(8,128)(2,1)}, bf16[1,2,512,2048]{3,2,1,0:T(8,128)(2,1)S(1)}, u32[]{:S(2)}) %copy-start) | copy-done | bytes 4194328
  26.6 0.0 copy-start.1
  26.6 0.6 copy-done.1
  27.2 129.5 %shard_map.96 = (bf16[1,2,512,2048]{3,2,1,0:T(8,128)(2,1)}, f32[2,4,64]{2,1,0:T(4,128)}) custom-call(bf16[1,2,512,2048]{3,2,1,0:T(8,128)(2,1)} %copy-done, f32[8,64]{1,0:T(8,128)} %copy-done.1), custom_call_target="tpu_custom_call" | custom-call | tf_op jit(solution)/shard_map/pallas_call | solution.py:423
Async XLA Ops:
  24.7 1.9 %copy-start = (bf16[1,2,512,2048]{3,2,1,0:T(8,128)(2,1)}, bf16[1,2,512,2048]{3,2,1,0:T(8,128)(2,1)S(1)}, u32[]{:S(2)}) copy-start(bf16[1,2,512,2048]{3,2,1,0:T(8,128)(2,1)S(1)} %get-tuple-element.6.multiples) | copy-start | bytes 12582916
  26.6 0.6 copy-start.1

commit v4 on v2

--- a/solution.py
+++ b/solution.py
@@ -50,9 +50,43 @@
     reader = pan * REP + rep
     me = freq * R + reader
 
-    def place(s):
-        r = lax.rem(s, R)
-        return {"freq": lax.div(s, R), "pan": lax.div(r, REP), "rep": lax.rem(r, REP)}
+    def turn(at, step, size):
+        return at if isinstance(step, int) and step == 0 else lax.rem(at + step, size)
+
+    pans = [turn(pan, k, PAN) for k in range(PAN)]
+    reps = [turn(rep, k, REP) for k in range(REP)]
+    back_pans = [turn(pan, PAN - k, PAN) if k else pan for k in range(PAN)]
+    back_reps = [turn(rep, REP - k, REP) if k else rep for k in range(REP)]
+
+    def each_peer(act):
+        def band(k):
+            there = turn(freq, k, NF)
+            back = freq if isinstance(k, int) and k == 0 else lax.rem(freq + NF - k, NF)
+            for dp in range(PAN):
+                for dr in range(REP):
+                    if isinstance(k, int) and (k, dp, dr) == (0, 0, 0):
+                        continue
+                    act(
+                        k * R + dp * REP + dr,
+                        (there, pans[dp], reps[dr]),
+                        (back, back_pans[dp], back_reps[dr]),
+                    )
+
+        band(0)
+        if N <= 32:
+            for k in range(1, NF):
+                band(k)
+        else:
+            pl.loop(1, NF)(band)
+
+    def place(spot):
+        return {"freq": spot[0], "pan": spot[1], "rep": spot[2]}
+
+    def number(spot):
+        return spot[0] * R + spot[1] * REP + spot[2]
+
+    def lane_block(spot):
+        return spot[0] * PAN + spot[1] if REP == PB else lax.div(number(spot), PB)
 
     loads = [
         pltpu.make_async_copy(panel_hbm, panel_s, load_sem.at[0]),
@@ -69,11 +103,11 @@
 
     barrier = pltpu.get_barrier_semaphore()
 
-    @pl.loop(1, N)
-    def _(k):
-        pl.semaphore_signal(
-            barrier, inc=1, device_id=place(lax.rem(me + k, N)), device_id_type=MESH
-        )
+    each_peer(
+        lambda k, target, source: pl.semaphore_signal(
+            barrier, inc=1, device_id=place(target), device_id_type=MESH
+        )
+    )
 
     loads[0].wait()
     loads[1].wait()
@@ -81,7 +115,7 @@
     offsets = [o for o in offsets if o[0]] + [o for o in offsets if not o[0]]
 
     for n, (dp, dr) in enumerate(offsets):
-        p = panel_s[lax.rem(pan + dp, PAN) * REP + lax.rem(rep + dr, REP), reader]
+        p = panel_s[pans[dp] * REP + reps[dr], reader]
         for c in range(CHUNKS):
             send[n, c] = data_v[:, p, :, c * W : (c + 1) * W]
     pl.semaphore_wait(barrier, N - 1)
@@ -93,7 +127,7 @@
             dst_ref=panels.at[c, :, slot],
             send_sem=send_sem.at[n, c],
             recv_sem=recv_sem.at[n, c],
-            device_id={"pan": lax.rem(pan + dp, PAN), "rep": lax.rem(rep + dr, REP)},
+            device_id={"pan": pans[dp], "rep": reps[dr]},
             device_id_type=MESH,
         )
 
@@ -208,7 +242,7 @@
     prepare(0)
     for c in range(CHUNKS):
         for n, (dp, dr) in enumerate(offsets):
-            sender = lax.rem(pan + PAN - dp, PAN) * REP + lax.rem(rep + REP - dr, REP)
+            sender = back_pans[dp] * REP + back_reps[dr]
             panel_copy(n, c, sender).wait_recv()
         pick(c)
         if c < CHUNKS - 1:
@@ -224,7 +258,7 @@
 
     def pick_copy(k, target, slot):
         return pltpu.make_async_remote_copy(
-            src_ref=picks.at[lax.div(target, PB)],
+            src_ref=picks.at[lane_block(target)],
             dst_ref=arrived.at[slot],
             send_sem=pick_send.at[k],
             recv_sem=pick_recv.at[k],
@@ -232,16 +266,10 @@
             device_id_type=MESH,
         )
 
-    @pl.loop(1, N)
-    def _(k):
-        pick_copy(k, lax.rem(me + k, N), me).start()
-
-    arrived[me] = picks[lax.div(me, PB)]
+    each_peer(lambda k, target, source: pick_copy(k, target, me).start())
+    arrived[me] = picks[lane_block((freq, pan, rep))]
     multiply(CHUNKS - 1)
-
-    @pl.loop(1, N)
-    def _(k):
-        pick_copy(k, lax.rem(me + k, N), lax.rem(me + N - k, N)).wait_recv()
+    each_peer(lambda k, target, source: pick_copy(k, target, number(source)).wait_recv())
 
     for j in range(NF):
         total = arrived[j * R]
@@ -249,16 +277,13 @@
             total = total + arrived[j * R + r]
         tidy[j : j + 1, :] = total[0:1]
         tidy[NF + j : NF + j + 1, :] = total[1:2]
-    part = lax.rem(me, PB)
+    part = rep if REP == PB else lax.rem(me, PB)
     value = tidy[:, :TL]
     for h in range(1, PB):
         value = jnp.where(part == h, tidy[:, h * TL : (h + 1) * TL], value)
     prim_v[...] = spectrum.astype(F32)[: 2 * NF] - value
 
-    @pl.loop(1, N)
-    def _(k):
-        pick_copy(k, lax.rem(me + k, N), me).wait_send()
-
+    each_peer(lambda k, target, source: pick_copy(k, target, me).wait_send())
     for c in range(CHUNKS):
         for n in range(R - 1):
             panel_copy(n, c, reader).wait_send()

time: 27.6 us -> 27.4 us (level)
  no operation moved by 1% of the time
where the time goes in v4:
time: 27.4 us; the launch traced here: 27.3 us
  Pallas kernels  24 us (88%)
  local copies, waits for them, and re-layouts  2.61 us (10%)
  between operations  0.64 us (2%)
    pallas_call x1, Pallas kernels, local(): pl.pallas_call(functools.partial(kernel, sizes), out_shape=(jax.ShapeDtyp...  24 us
    unnamed x2, local copies, waits for them, and re-layouts  2.61 us

profile of v4, /device:TPU:0, one launch (start us, length us, event | category | flops | bytes accessed | tf_op | source)
XLA Modules:
  0.0 27.3 jit_solution(10893982418643740781)
XLA Ops:
  0.6 24.0 %shard_map.95 = (bf16[1,2,512,2048]{3,2,1,0:T(8,128)(2,1)S(1)}, f32[8,64]{1,0:T(8,128)S(1)}) custom-call(bf16[1,2,16,32,2048]{4,3,2,1,0:T(8,128)(2,1)} %bitcast.7, bf16[64,4096]{1,0:T(8,128)(2,1)} %traces_hbm.1, bf16[16,4096]{1,0:T(8,128)(2,1)} %constant.2.clone.table_hbm, s32[4,4]{1,0:T(4,128)} %panel_hbm.1, s32[4,4]{1,0:T(4,128)} %order_hbm.1, ...), custom_call_target="tpu_custom_call" | custom-call | tf_op jit(solution)/shard_map/pallas_call | solution.py:309
  24.6 2.0 %copy.12 = bf16[1,2,512,2048]{3,2,1,0:T(8,128)(2,1)} copy(bf16[1,2,512,2048]{3,2,1,0:T(8,128)(2,1)S(1)} %get-tuple-element.8) | data formatting | bytes 8388608
  26.7 0.6 %copy.13 = f32[64,2,4]{0,2,1:T(4,128)} copy(f32[64,2,4]{0,2,1:T(4,128)S(1)} %bitcast.6) | data formatting | bytes 4096

commit v5 on v4

--- a/solution.py
+++ b/solution.py
@@ -156,15 +156,17 @@
         rows = lax.broadcasted_iota(jnp.int32, (256, RK), 0) + at
         sel[pl.ds(at, 256), :] = jnp.where(rows == column, 1.0, 0.0).astype(BF)
 
-    @pl.loop(0, SW // 128)
+    BAND = min(SW, 512)
+
+    @pl.loop(0, SW // BAND)
     def _(b):
-        rows = pl.ds(pl.multiple_of(b * 128, 128), 128)
-        strips = pl.ds(b * (128 // KB), 128 // KB)
+        rows = pl.ds(pl.multiple_of(b * BAND, BAND), BAND)
+        strips = pl.ds(b * (BAND // KB), BAND // KB)
         real = jnp.dot(
-            data_v[0, strips].reshape(128, NS), sel[...], preferred_element_type=F32
+            data_v[0, strips].reshape(BAND, NS), sel[...], preferred_element_type=F32
         )
         imag = jnp.dot(
-            data_v[1, strips].reshape(128, NS), sel[...], preferred_element_type=F32
+            data_v[1, strips].reshape(BAND, NS), sel[...], preferred_element_type=F32
         )
         left_a[rows, :RK] = real.astype(BF)
         left_a[rows, RK:] = (-imag).astype(BF)

time: 27.4 us -> 27.4 us (level)
  no operation moved by 1% of the time
where the time goes in v5:
time: 27.4 us; the launch traced here: 27.3 us
  Pallas kernels  24 us (88%)
  local copies, waits for them, and re-layouts  2.61 us (10%)
  between operations  0.64 us (2%)
    pallas_call x1, Pallas kernels, local(): pl.pallas_call(functools.partial(kernel, sizes), out_shape=(jax.ShapeDtyp...  24 us
    unnamed x2, local copies, waits for them, and re-layouts  2.61 us

profile of v5, /device:TPU:0, one launch (start us, length us, event | category | flops | bytes accessed | tf_op | source)
XLA Modules:
  0.0 27.3 jit_solution(146450300877441356)
XLA Ops:
  0.6 24.0 %shard_map.95 = (bf16[1,2,512,2048]{3,2,1,0:T(8,128)(2,1)S(1)}, f32[8,64]{1,0:T(8,128)S(1)}) custom-call(bf16[1,2,16,32,2048]{4,3,2,1,0:T(8,128)(2,1)} %bitcast.7, bf16[64,4096]{1,0:T(8,128)(2,1)} %traces_hbm.1, bf16[16,4096]{1,0:T(8,128)(2,1)} %constant.2.clone.table_hbm, s32[4,4]{1,0:T(4,128)} %panel_hbm.1, s32[4,4]{1,0:T(4,128)} %order_hbm.1, ...), custom_call_target="tpu_custom_call" | custom-call | tf_op jit(solution)/shard_map/pallas_call | solution.py:311
  24.6 2.0 %copy.12 = bf16[1,2,512,2048]{3,2,1,0:T(8,128)(2,1)} copy(bf16[1,2,512,2048]{3,2,1,0:T(8,128)(2,1)S(1)} %get-tuple-element.8) | data formatting | bytes 8388608
  26.7 0.6 %copy.13 = f32[64,2,4]{0,2,1:T(4,128)} copy(f32[64,2,4]{0,2,1:T(4,128)S(1)} %bitcast.6) | data formatting | bytes 4096
